TPU v7x, 512 devices: a whole 4x8x8 slice. The times are simulated.
512 devices in a mesh: band: 64 (over z, y), lev: 8 (over x, core).
Axes of the slice: x: 4, y: 8, z: 8, core: 2. Of those that a mesh axis runs over, the one named last changes fastest.
Arguments:
- fourier: bfloat16 [24, 4, 2560, 256], P('lev', None, 'band'), may hold values from -6 to 6
- cycle_points: int32 [2560], P('band'), may hold values from 16 to 5144, as said below
- lat_weight: float32 [2560], P('band'), may hold values from 0.3 to 3
- wave_m: int32 [256], replicated, may hold values from 0 to 1279, as said below
- legendre: bfloat16 [256, 1280, 2560], P('band', 'lev'), may hold values from -0.125 to 0.125
- diffusion: float32 [24], replicated, may hold values from 0.5 to 8
- mode_forward: bfloat16 [24, 24], replicated, may hold values from -1.25 to 1.25
- mode_back: bfloat16 [24, 24], replicated, may hold values from -1.25 to 1.25
- mode_depth: float32 [24], replicated, may hold values from 0.2 to 5
Outputs:
- fourier_new: bfloat16 [24, 4, 2560, 256], P('lev', None, 'band')
Inputs may be any that keep to these rules, and one draw needn't show every extreme that they name: `wave_m`: distinct zonal wavenumbers; slot s belongs to the band device of index s // 4; both 0 and 1279 occur. `cycle_points`: a multiple of 4; 16 on the two polar cycles.
All inputs are finite; a program needn't handle non-finite values.
Results may differ from a plain program's by a relative error of at most 0.0062.
Values may be sent and summed in bfloat16 or wider, within the bound.
A program may use at most 128 MiB of HBM per device.

v0:
```python
import jax
import jax.numpy as jnp
from jax import lax
from jax.sharding import PartitionSpec as P


def legendre_direct(fields, legendre):
    return jnp.einsum("lcps,sjp->lcsj", fields, legendre, preferred_element_type=jnp.float32)


def legendre_inverse(fields, legendre):
    return jnp.einsum("lcsj,sjp->lcps", fields, legendre, preferred_element_type=jnp.float32)


def on_device(
    fourier,
    cycle_points,
    lat_weight,
    wave_m,
    legendre,
    diffusion,
    mode_forward,
    mode_back,
    mode_depth,
):
    own_slots = legendre.shape[0]
    columns = legendre.shape[1]
    level_count = lax.axis_size("lev")
    degrees_all = columns * level_count
    band_index = lax.axis_index("band")
    lev_index = lax.axis_index("lev")
    present_cycles = (wave_m[None, :] < (cycle_points // 2)[:, None]).astype(jnp.float32)
    weighted = (
        fourier.astype(jnp.float32) * lat_weight[None, None, :, None] * present_cycles[None, None]
    ).astype(jnp.bfloat16)
    own_waves = lax.dynamic_slice_in_dim(wave_m, band_index * own_slots, own_slots)
    degree = (
        own_waves[:, None] + lev_index * columns + jnp.arange(columns, dtype=jnp.int32)[None, :]
    )
    usable = (degree <= degrees_all - 1).astype(jnp.float32)
    degree_float = degree.astype(jnp.float32)
    degree_ratio = degree_float * (degree_float + 1.0) / float(degrees_all * (degrees_all - 1))
    exchanged = lax.all_to_all(weighted, "band", split_axis=3, concat_axis=2, tiled=True)
    summed = legendre_direct(lax.all_gather(exchanged, "lev", axis=0, tiled=True), legendre)
    spectral = (summed * usable[None, None]).astype(jnp.bfloat16)
    damping = 1.0 + diffusion[:, None, None, None] * (degree_ratio * degree_ratio)[None, None]
    vorticity = spectral[:, 0:2].astype(jnp.float32) / damping
    modes = jnp.einsum(
        "kl,lcsj->kcsj", mode_forward, spectral[:, 2:4], preferred_element_type=jnp.float32
    )
    scaled = (
        modes / (1.0 + 4.0 * mode_depth[:, None, None, None] * degree_ratio[None, None])
    ).astype(jnp.bfloat16)
    new_div = jnp.einsum("lk,kcsj->lcsj", mode_back, scaled, preferred_element_type=jnp.float32)
    updated = jnp.concatenate([vorticity, new_div], axis=1).astype(jnp.bfloat16)
    summed = lax.psum_scatter(
        legendre_inverse(updated, legendre), "lev", scatter_dimension=0, tiled=True
    )
    gridded = summed.astype(jnp.bfloat16)
    returned = lax.all_to_all(gridded, "band", split_axis=2, concat_axis=3, tiled=True)
    return returned * present_cycles[None, None].astype(jnp.bfloat16)


def solution(mesh):
    placed = (
        P("lev", None, "band", None),
        P("band"),
        P("band"),
        P(),
        P("band", "lev", None),
        P(),
        P(),
        P(),
        P(),
    )
    return jax.shard_map(
        on_device,
        mesh=mesh,
        in_specs=placed,
        out_specs=P("lev", None, "band", None),
        check_vma=False,
    )
```

profile of v0, /device:TPU:1, one launch (start us, length us, event | category | flops | bytes accessed | tf_op | source)
XLA Modules:
  0.0 224.8 jit_solution(3707644353623002173)
XLA Ops:
  6.5 0.0 copy-start
  6.5 0.0 all-gather.2.cloned.1.call-start
  6.5 0.8 and_select_fusion
  7.4 1.5 fusion.27
  8.9 1.1 multiply_convert_fusion
  9.9 1.2 copy.43
  11.2 2.0 reshape.130
  13.2 0.0 copy-start.3
  13.2 0.0 copy-start.6
  13.3 0.0 copy-start.4
  13.3 29.8 %all_to_all.36 = bf16[64,2,960]{2,1,0:T(2,128)(2,1)} all-to-all(bf16[64,2,960]{2,1,0:T(2,128)(2,1)S(1)} %reshape.130), channel_id=1, replica_groups=mesh['band'=64,'lev'=8] {'band'}, dimensions={0} | all-to-all | bytes 491520 | tf_op jit(solution)/shard_map/all_to_all | solution.py:43
  43.1 2.8 %reshape.131 = bf16[256,3,4,40]{3,2,1,0:T(4,128)(2,1)} reshape(bf16[64,2,960]{2,1,0:T(2,128)(2,1)} %all_to_all.36) | data formatting | bytes 491520
  45.9 1.3 copy.44
  47.2 1.1 copy.45
  48.3 3.0 %all_to_all.29 = bf16[3,4,2560,4]{2,3,1,0:T(4,128)(2,1)} reshape(bf16[3,4,64,40,4]{3,2,4,1,0:T(8,128)(2,1)} %copy.45) | data formatting | bytes 491520 | tf_op jit(solution)/shard_map/all_to_all | solution.py:43
  51.2 0.0 all-gather.2.cloned.1.call-update
  51.3 1.3 dynamic-slice
  53.2 0.0 copy-done.3
  53.2 0.1 dynamic-slice_add_fusion
  53.3 0.0 copy-done.6
  53.3 0.1 fusion.32
  53.4 0.1 fusion.33
  53.4 0.0 copy-done.4
  53.4 0.1 multiply_add_fusion
  53.5 0.0 copy-start.5
  53.5 0.0 copy-start.2
  53.6 23.3 %all-gather.2.cloned.1.call-done = bf16[24,4,2560,4]{2,3,1,0:T(4,128)(2,1)} async-done(((bf16[3,4,2560,4]{2,3,1,0:T(4,128)(2,1)}), bf16[24,4,2560,4]{2,3,1,0:T(4,128)(2,1)}) %all-gather.2.cloned.1.call-update) | async-done | bytes 1966096 | tf_op jit(solution)/shard_map/all_gather | solution.py:44
  76.9 0.0 copy-done
  76.9 3.3 %fusion.15 = bf16[24,4,4,160]{3,0,1,2:T(8,128)(2,1)S(1)} fusion(bf16[4,160,2560]{2,1,0:T(8,128)(2,1)S(1)} %copy-done, bf16[24,4,2560,4]{2,3,1,0:T(4,128)(2,1)} %all-gather.2.cloned.1.call-done, f32[4,160]{1,0:T(4,128)S(1)} %fusion.32), kind=kOutput, calls=%fused_computation.9 | convolution fusion | flops 314695680 | bytes 5368320 | tf_op jit(solution)/shard_map/lcps,sjp->lcsj/dot_general | solution.py:8
  80.2 0.0 copy-done.5
  80.2 0.2 fusion.20
  80.3 0.0 copy-done.2
  80.4 0.2 fusion.21
  80.5 0.7 convolution_bitcast_fusion
  81.3 4.4 %copy.49 = f32[24,4,2560,4]{2,3,1,0:T(4,128)} copy(f32[24,4,2560,4]{2,0,1,3:T(8,128)S(1)} %convolution_bitcast_fusion) | data formatting | bytes 7864320 | tf_op jit(solution)/shard_map/lcsj,sjp->lcps/transpose | solution.py:12
  85.7 55.5 %all-reduce.2 = bf16[24,4,2560,4]{2,3,1,0:T(4,128)(2,1)} all-reduce(f32[24,4,2560,4]{2,3,1,0:T(4,128)} %copy.49), channel_id=2, replica_groups=mesh['band'=64,'lev'=8] {'lev'}, use_global_device_ids=true, to_apply=%region_0.1.clone | all-reduce | flops 983040 | bytes 5898240
  141.1 1.0 dynamic-slice_convert_fusion
  142.2 7.9 %copy.50 = bf16[3,4,2560,4]{3,1,0,2:T(4,128)(2,1)} copy(bf16[3,4,2560,4]{2,3,1,0:T(4,128)(2,1)S(1)} %dynamic-slice_convert_fusion) | data formatting | bytes 491520 | tf_op jit(solution)/shard_map/convert_element_type | solution.py:59
  150.1 15.9 %reshape.132 = bf16[64,2,960]{2,1,0:T(2,128)(2,1)} reshape(bf16[2560,3,4,4]{3,2,1,0:T(4,128)(2,1)} %bitcast.48) | data formatting | bytes 491520
  166.0 13.0 %all-to-all-start.1 = ((bf16[64,2,960]{2,1,0:T(2,128)(2,1)}), bf16[64,2,960]{2,1,0:T(2,128)(2,1)S(1)}, u32[]{:S(2)}, u32[]{:S(2)}) async-start(bf16[64,2,960]{2,1,0:T(2,128)(2,1)} %reshape.132), calls=%async_computation.1 | async-start | bytes 524288 | tf_op jit(solution)/shard_map/all_to_all | solution.py:60
  179.0 1.5 copy.53
  180.5 11.1 %all-to-all-done.1 = bf16[64,2,960]{2,1,0:T(2,128)(2,1)S(1)} async-done(((bf16[64,2,960]{2,1,0:T(2,128)(2,1)}), bf16[64,2,960]{2,1,0:T(2,128)(2,1)S(1)}, u32[]{:S(2)}, u32[]{:S(2)}) %all-to-all-start.1) | async-done | bytes 245792 | tf_op jit(solution)/shard_map/all_to_all | solution.py:60
  191.6 10.2 %reshape.133 = bf16[2560,3,4,4]{3,2,1,0:T(4,128)(2,1)} reshape(bf16[64,2,960]{2,1,0:T(2,128)(2,1)S(1)} %all-to-all-done.1) | data formatting | bytes 491520
  201.7 0.0 copy-start.1
  201.7 11.5 %copy.57 = bf16[3,4,64,40,4]{3,2,4,1,0:T(8,128)(2,1)} copy(bf16[3,4,64,40,4]{4,1,0,3,2:T(4,128)(2,1)} %bitcast.49) | data formatting | bytes 491520 | tf_op jit(solution)/shard_map/all_to_all | solution.py:60
  213.2 1.8 copy.52
  215.0 0.0 copy-done.1
  215.0 0.9 broadcast_multiply_fusion
  215.9 2.1 copy.54
  (2 shorter events, 0.0 us)
Async XLA Ops:
  6.5 70.4 %copy-start = (bf16[4,160,2560]{2,1,0:T(8,128)(2,1)S(1)}, bf16[4,160,2560]{2,1,0:T(8,128)(2,1)}, u32[]{:S(2)}) copy-start(bf16[4,160,2560]{2,1,0:T(8,128)(2,1)} %param.13) | copy-start | bytes 9830404
  6.5 70.3 %all-gather.2.cloned.1.call-start = ((), (), s32[]{:S(2)}) async-start(), calls=%async_computation.2 | async-start | bytes 2211840 | tf_op jit(solution)/shard_map/all_gather | solution.py:44
  13.2 40.0 %copy-start.3 = (s32[256]{0:T(256)S(1)}, s32[256]{0:T(256)}, u32[]{:S(2)}) copy-start(s32[256]{0:T(256)} %param.12) | copy-start | bytes 3076
  13.2 40.0 %copy-start.6 = (f32[24]{0:T(128)S(1)}, f32[24]{0:T(128)}, u32[]{:S(2)}) copy-start(f32[24]{0:T(128)} %param.17) | copy-start | bytes 292
  13.3 40.2 %copy-start.4 = (f32[24]{0:T(128)S(1)}, f32[24]{0:T(128)}, u32[]{:S(2)}) copy-start(f32[24]{0:T(128)} %param.14) | copy-start | bytes 292
  53.5 26.6 %copy-start.5 = (bf16[24,24]{1,0:T(8,128)(2,1)S(1)}, bf16[24,24]{1,0:T(8,128)(2,1)}, u32[]{:S(2)}) copy-start(bf16[24,24]{1,0:T(8,128)(2,1)} %param.15) | copy-start | bytes 3460
  53.5 26.8 %copy-start.2 = (bf16[24,24]{1,0:T(8,128)(2,1)S(1)}, bf16[24,24]{1,0:T(8,128)(2,1)}, u32[]{:S(2)}) copy-start(bf16[24,24]{1,0:T(8,128)(2,1)} %param.16) | copy-start | bytes 3460
  166.0 25.6 %all-to-all-start.1 = ((bf16[64,2,960]{2,1,0:T(2,128)(2,1)}), bf16[64,2,960]{2,1,0:T(2,128)(2,1)S(1)}, u32[]{:S(2)}, u32[]{:S(2)}) async-start(bf16[64,2,960]{2,1,0:T(2,128)(2,1)} %reshape.132), calls=%async_computation.1 | async-start | bytes 524288 | tf_op jit(solution)/shard_map/all_to_all | solution.py:60
  201.7 13.3 %copy-start.1 = (bf16[40,256]{0,1:T(8,128)(2,1)S(1)}, bf16[40,256]{0,1:T(8,128)(2,1)}, u32[]{:S(2)}) copy-start(bf16[40,256]{0,1:T(8,128)(2,1)} %copy.53) | copy-start | bytes 61444
Sparse Core Ops, SparseCore 0:
  51.4 25.4 all-gather.1
where the time goes:
time: 227 us; the launch traced here: 225 us
  blocking collectives  85.3 us (38%)
  local copies, waits for them, and re-layouts  69 us (30%)
  waiting for transfers between devices  34.4 us (15%)
  between operations  14.2 us (6%)
  starting transfers between devices  13 us (6%)
  other arithmetic  4.68 us (2%)
  matrix products  4.31 us (2%)
    unnamed x1, blocking collectives  55.5 us
    unnamed x19, local copies, waits for them, and re-layouts  32.3 us
    all_to_all x1, blocking collectives, on_device(): lax.all_to_all(weighted, 'band', split_axis=3, concat_axis=2, tiled=True)  29.8 us
    all_gather x1, waiting for transfers between devices, on_device(): lax.all_gather(exchanged, 'lev', axis=0, tiled=True)  23.3 us
    all_to_all x2, local copies, waits for them, and re-layouts, on_device(): lax.all_to_all(gridded, 'band', split_axis=2, concat_axis=3, tiled=True)  13.2 us
    all_to_all x1, starting transfers between devices, on_device(): lax.all_to_all(gridded, 'band', split_axis=2, concat_axis=3, tiled=True)  13 us
    all_to_all x1, waiting for transfers between devices, on_device(): lax.all_to_all(gridded, 'band', split_axis=2, concat_axis=3, tiled=True)  11.1 us
    convert_element_type x2, local copies, waits for them, and re-layouts, on_device(): gridded = summed.astype(jnp.bfloat16)  8.95 us
  transfers between devices with their start and end apart: 2, of which 2 were waited for; matrix products, arithmetic and copies ran while one was open for 1% of the time, Pallas kernels for 0%

commit v1 on v0

v1 whole, which is shorter than its diff:
```python
import functools
import jax
import jax.numpy as jnp
from jax import lax
from jax.sharding import PartitionSpec as P
from jax.experimental import pallas as pl
from jax.experimental.pallas import tpu as pltpu

F32 = jnp.float32
BF16 = jnp.bfloat16
MESH = pl.DeviceIdType.MESH

LEV3 = 3
COMP = 4
CYC = 40
BANDS = 64
LEVS = 8
CHIPS = 4
GROUP = 16
GROUPS = 4
WIDE = GROUP * CYC
ROWS = 48
DEG = 160
SLOTS = 4
NSPEC = 1280


def iota(shape, dim):
    return lax.broadcasted_iota(jnp.int32, shape, dim)


def column_of(row, count):
    same = iota((count, count), 0) == iota((count, count), 1)
    return jnp.sum(jnp.where(same, row, 0.0), axis=1, keepdims=True)


def kernel(
    four, cyc, latw, wave, leg_hbm, diff, mf, mb, depth, out,
    leg, tmp, send, r1, xall, acc, ut, gf, gb, grecv,
    t1s, t1r, fms, fmr, fps, fpr, esend, r2,
    leg_sem, r1_send, r1_recv, x_send, l_recv, r_recv, far_recv, sib_recv,
    gx_send, gx_recv, t1_send, t1_recv, fm_send, fm_recv, fp_send, fp_recv,
    e_send, r2_recv,
):
    band = lax.axis_index("band")
    lev = lax.axis_index("lev")
    x = lev // 2
    core = lev % 2
    qme = band // GROUP
    right = lax.rem(x + 1, CHIPS) * 2 + core
    left = lax.rem(x + 3, CHIPS) * 2 + core
    far = lax.rem(x + 2, CHIPS) * 2 + core
    sib = x * 2 + 1 - core

    def to_lev(src, dst, s_sem, r_sem, target):
        pltpu.make_async_remote_copy(
            src_ref=src, dst_ref=dst, send_sem=s_sem, recv_sem=r_sem,
            device_id={"lev": target}, device_id_type=MESH,
        ).start()

    def wait_bytes(ref, sem):
        pltpu.make_async_copy(ref, ref, sem).wait()

    barrier = pltpu.get_barrier_semaphore()

    def greet(i, carry):
        pl.semaphore_signal(
            barrier, inc=1, device_id={"band": lax.rem(band + i, BANDS)}, device_id_type=MESH
        )
        return carry

    lax.fori_loop(1, BANDS, greet, 0)
    for other in (right, left, sib):
        pl.semaphore_signal(barrier, inc=1, device_id={"lev": other}, device_id_type=MESH)

    for q in range(GROUPS):
        pltpu.make_async_copy(
            leg_hbm.at[:, pl.ds(q * WIDE, WIDE)], leg.at[q], leg_sem.at[q]
        ).start()

    half = column_of((cyc[...] // 2).astype(F32), CYC)
    weight = column_of(latw[...], CYC)
    waves = wave[...].astype(F32)
    present = waves < half
    scale = jnp.where(present, weight, 0.0)
    for c in range(COMP):
        parts = [four[l, c].astype(F32) * scale for l in range(LEV3)]
        parts.append(jnp.zeros((8, 256), F32))
        tmp[pl.ds(c, 256, stride=4), :] = jnp.concatenate(parts, axis=0).T
    send[...] = tmp[...].reshape(BANDS, 16, 128).astype(BF16)

    pl.semaphore_wait(barrier, BANDS - 1 + 3)

    def scatter(i, carry):
        t = i // GROUP
        turn = t + (t // 2) * (5 - 2 * t)
        there = lax.rem(qme + 4 - turn, GROUPS) * GROUP + lax.rem(band + i, GROUP)

        @pl.when(there != band)
        def _():
            pltpu.make_async_remote_copy(
                src_ref=send.at[there], dst_ref=r1.at[band],
                send_sem=r1_send, recv_sem=r1_recv.at[qme],
                device_id={"band": there}, device_id_type=MESH,
            ).start()

        @pl.when(there == band)
        def _():
            pltpu.make_async_copy(send.at[band], r1.at[band], r1_recv.at[qme]).start()

        return carry

    lax.fori_loop(0, BANDS, scatter, 0)

    cols = LEVS * LEV3 * COMP
    rows = LEVS * ROWS
    levels = LEVS * LEV3
    pick_k = (iota((cols, levels), 0) // COMP == iota((cols, levels), 1)).astype(BF16)
    pick_l = (iota((rows, levels), 0) // 16 == iota((rows, levels), 1)).astype(BF16)
    spread = lax.dot_general(pick_k, mf[...], (((1,), (0,)), ((), ())), preferred_element_type=F32)
    spread = lax.dot_general(
        spread.astype(BF16), pick_l, (((1,), (1,)), ((), ())), preferred_element_type=F32
    )
    row_c = iota((cols, rows), 0) % COMP
    col_c = iota((cols, rows), 1) % COMP
    same_level = iota((cols, rows), 0) // COMP == iota((cols, rows), 1) // 16
    forward = jnp.where(
        row_c == col_c,
        jnp.where(row_c < 2, same_level.astype(F32), spread), 0.0,
    ).astype(BF16)
    back = lax.dot_general(pick_l, mb[...], (((1,), (0,)), ((), ())), preferred_element_type=F32)
    back = lax.dot_general(
        back.astype(BF16), pick_k, (((1,), (1,)), ((), ())), preferred_element_type=F32
    )
    row_b = iota((rows, cols), 0) % COMP
    col_b = iota((rows, cols), 1) % COMP
    same_back = iota((rows, cols), 0) // 16 == iota((rows, cols), 1) // COMP
    backward = jnp.where(
        row_b == col_b,
        jnp.where(row_b < 2, same_back.astype(F32), back), 0.0,
    ).astype(BF16)
    pick_f = iota((cols, levels), 0) // COMP == iota((cols, levels), 1)
    diff_col = jnp.sum(jnp.where(pick_f, diff[...], 0.0), axis=1, keepdims=True)
    depth_col = jnp.sum(jnp.where(pick_f, depth[...], 0.0), axis=1, keepdims=True)
    lane = iota((1, SLOTS * DEG), 1)
    slot_of = lane // DEG
    own = jnp.zeros((1, SLOTS * DEG), F32)
    for s in range(SLOTS):
        mine = iota((1, 256), 1) == band * SLOTS + s
        wave_s = jnp.sum(jnp.where(mine, waves, 0.0), axis=1, keepdims=True)
        own = jnp.where(slot_of == s, wave_s, own)
    degree = own + (lane % DEG + lev * DEG).astype(F32)
    usable = degree <= float(NSPEC - 1)
    ratio = degree * (degree + 1.0) / float(NSPEC * (NSPEC - 1))
    row_col = iota((cols, 1), 0) % COMP
    damping = jnp.where(
        row_col < 2, 1.0 + diff_col * (ratio * ratio), 1.0 + 4.0 * depth_col * ratio
    )

    lane16 = iota((16, 128), 1)

    def turn_of(n):
        t = n + (n // 2) * (5 - 2 * n)
        return lax.rem(qme + t, GROUPS)

    def take(n):
        q = turn_of(n)
        wait_bytes(r1.at[pl.ds(q * GROUP, GROUP)], r1_recv.at[q])
        mine = xall.at[q * LEVS + lev]
        tiles = [r1[q * GROUP + i].astype(F32) for i in range(GROUP)]
        for l in range(LEV3):
            for t in range(WIDE // 128):
                value = None
                for i in range(GROUP):
                    low = CYC * i - 128 * t
                    if low + CYC <= 0 or low >= 128:
                        continue
                    shift = (low - CYC * l) % 128
                    moved = pltpu.roll(tiles[i], shift, 1) if shift else tiles[i]
                    value = moved if value is None else jnp.where(lane16 >= low, moved, value)
                mine[pl.ds(16 * l, 16), pl.ds(128 * t, 128)] = value.astype(BF16)
        to_lev(mine, mine, x_send.at[q], l_recv.at[q], right)
        to_lev(mine, mine, x_send.at[q], r_recv.at[q], left)
        to_lev(mine, mine, x_send.at[q], sib_recv.at[q], sib)

    def relay(n):
        q = turn_of(n)
        from_left = xall.at[q * LEVS + left]
        from_right = xall.at[q * LEVS + right]
        wait_bytes(from_left, l_recv.at[q])
        wait_bytes(from_right, r_recv.at[q])
        onward = q % 2

        @pl.when(onward == 0)
        def _():
            to_lev(from_left, from_left, x_send.at[q], far_recv.at[q], right)

        @pl.when(onward == 1)
        def _():
            to_lev(from_right, from_right, x_send.at[q], far_recv.at[q], left)

        to_lev(from_left, from_left, x_send.at[q], sib_recv.at[q], sib)
        to_lev(from_right, from_right, x_send.at[q], sib_recv.at[q], sib)

    def relay_far(n):
        q = turn_of(n)
        from_far = xall.at[q * LEVS + far]
        wait_bytes(from_far, far_recv.at[q])
        to_lev(from_far, from_far, x_send.at[q], sib_recv.at[q], sib)

    def multiply(n):
        q = turn_of(n)
        wait_bytes(xall.at[pl.ds(0, 4)], sib_recv.at[q])
        wait_bytes(leg.at[q], leg_sem.at[q])
        fields = xall[pl.ds(q * LEVS, LEVS)].reshape(rows, WIDE)
        term = lax.dot_general(
            fields, leg[q], (((1,), (1,)), ((), ())), preferred_element_type=F32
        )

        @pl.when(n == 0)
        def _():
            acc[...] = term

        @pl.when(n > 0)
        def _():
            acc[...] += term

    def direct(n, carry):
        pl.when(n < GROUPS)(lambda: take(n))
        pl.when((n >= 1) & (n < GROUPS + 1))(lambda: relay(n - 1))
        pl.when((n >= 2) & (n < GROUPS + 2))(lambda: relay_far(n - 2))
        pl.when(n >= 3)(lambda: multiply(n - 3))
        return carry

    lax.fori_loop(0, GROUPS + 3, direct, 0)

    own_slot = (iota((rows, 1), 0) // COMP) % SLOTS == slot_of
    spectral = jnp.where(own_slot & usable, acc[...], 0.0).astype(BF16)
    modes = jnp.dot(forward, spectral, preferred_element_type=F32)
    scaled = (modes / damping).astype(BF16)
    updated = jnp.dot(backward, scaled, preferred_element_type=F32)
    ut[...] = jnp.where(own_slot, updated, 0.0).astype(BF16)

    def out_of(n):
        t = (GROUPS - 1) - n
        t = t + (t // 2) * (5 - 2 * t)
        return lax.rem(qme + t, GROUPS)

    def ahead_of(q):
        sense = 1 + 2 * (q % 2)
        ahead = lax.rem(x + sense, CHIPS)
        behind = lax.rem(x + 4 - sense, CHIPS)
        return ahead, behind

    def inverse(n):
        q = out_of(n)
        sums = jnp.dot(ut[...], leg[q], preferred_element_type=F32)
        gf[q] = sums.reshape(LEVS, ROWS, WIDE)
        gb[q] = sums.astype(BF16).reshape(CHIPS, 2, ROWS, WIDE)
        to_lev(gb.at[q, :, 1 - core], grecv.at[q], gx_send.at[q], gx_recv.at[q], sib)

    def chip_sum(q, target):
        return gf[q, target * 2 + core] + grecv[q, target].astype(F32)

    def first_hop(n):
        q = out_of(n)
        wait_bytes(grecv.at[q], gx_recv.at[q])
        ahead, behind = ahead_of(q)
        opposite = lax.rem(x + 2, CHIPS)
        t1s[q] = chip_sum(q, opposite).astype(BF16)
        to_lev(t1s.at[q], t1r.at[q], t1_send.at[q], t1_recv.at[q], ahead * 2 + core)
        fms[q] = chip_sum(q, behind).astype(BF16)
        to_lev(fms.at[q], fmr.at[q], fm_send.at[q], fm_recv.at[q], behind * 2 + core)

    def second_hop(n):
        q = out_of(n)
        ahead, behind = ahead_of(q)
        wait_bytes(t1r.at[q], t1_recv.at[q])
        fps[q] = (chip_sum(q, ahead) + t1r[q].astype(F32)).astype(BF16)
        to_lev(fps.at[q], fpr.at[q], fp_send.at[q], fp_recv.at[q], ahead * 2 + core)

    def give(n):
        q = out_of(n)
        wait_bytes(fmr.at[q], fm_recv.at[q])
        wait_bytes(fpr.at[q], fp_recv.at[q])
        total = chip_sum(q, x) + fmr[q].astype(F32) + fpr[q].astype(F32)
        for i in range(GROUP):
            t, low = divmod(CYC * i, 128)
            value = None
            for l in range(LEV3):
                piece = total[16 * l:16 * l + 16, 128 * t:128 * t + 128]
                shift = (CYC * l - low) % 128
                moved = pltpu.roll(piece, shift, 1) if shift else piece
                if low + CYC > 128:
                    beyond = total[16 * l:16 * l + 16, 128 * t + 128:128 * t + 256]
                    after = pltpu.roll(beyond, shift, 1) if shift else beyond
                    moved = jnp.where(lane16 >= CYC * l + 128 - low, after, moved)
                value = moved if value is None else jnp.where(lane16 >= CYC * l, moved, value)
            esend[q * GROUP + i] = value.astype(BF16)

        def deliver(i, carry):
            there = q * GROUP + lax.rem(band + i, GROUP)

            @pl.when(there != band)
            def _():
                pltpu.make_async_remote_copy(
                    src_ref=esend.at[there], dst_ref=r2.at[band],
                    send_sem=e_send, recv_sem=r2_recv,
                    device_id={"band": there}, device_id_type=MESH,
                ).start()

            @pl.when(there == band)
            def _():
                pltpu.make_async_copy(esend.at[band], r2.at[band], r2_recv).start()

            return carry

        lax.fori_loop(0, GROUP, deliver, 0)

    def back_transform(n, carry):
        pl.when(n < GROUPS)(lambda: inverse(n))
        pl.when((n >= 1) & (n < GROUPS + 1))(lambda: first_hop(n - 1))
        pl.when((n >= 2) & (n < GROUPS + 2))(lambda: second_hop(n - 2))
        pl.when(n >= 3)(lambda: give(n - 3))
        return carry

    lax.fori_loop(0, GROUPS + 3, back_transform, 0)

    wait_bytes(r2, r2_recv)
    tmp[...] = r2[...].astype(F32).reshape(BANDS * 16, 128)
    for c in range(COMP):
        turned = tmp[pl.ds(c, 256, stride=4), :].T
        for l in range(LEV3):
            out[l, c] = jnp.where(present, turned[CYC * l:CYC * l + CYC], 0.0).astype(BF16)

    wait_bytes(send.at[pl.ds(0, BANDS - 1)], r1_send)
    wait_bytes(esend.at[pl.ds(0, BANDS - 1)], e_send)
    for q in range(GROUPS):
        wait_bytes(xall.at[pl.ds(0, 7)], x_send.at[q])
        wait_bytes(grecv.at[q], gx_send.at[q])
        wait_bytes(t1s.at[q], t1_send.at[q])
        wait_bytes(fms.at[q], fm_send.at[q])
        wait_bytes(fps.at[q], fp_send.at[q])


def on_device(
    fourier, cycle_points, lat_weight, wave_m, legendre, diffusion, mode_forward, mode_back,
    mode_depth,
):
    vmem = pl.BlockSpec(memory_space=pltpu.VMEM)
    piece = (GROUPS, ROWS, WIDE)
    dma = pltpu.SemaphoreType.DMA
    return pl.pallas_call(
        kernel,
        out_shape=jax.ShapeDtypeStruct(fourier.shape, BF16),
        in_specs=[vmem] * 4 + [pl.BlockSpec(memory_space=pl.ANY)] + [vmem] * 4,
        out_specs=vmem,
        scratch_shapes=[
            pltpu.VMEM((GROUPS, SLOTS * DEG, WIDE), BF16),
            pltpu.VMEM((BANDS * 16, 128), F32),
            pltpu.VMEM((BANDS, 16, 128), BF16),
            pltpu.VMEM((BANDS, 16, 128), BF16),
            pltpu.VMEM((GROUPS * LEVS, ROWS, WIDE), BF16),
            pltpu.VMEM((LEVS * ROWS, SLOTS * DEG), F32),
            pltpu.VMEM((LEVS * ROWS, SLOTS * DEG), BF16),
            pltpu.VMEM((GROUPS, LEVS, ROWS, WIDE), F32),
            pltpu.VMEM((GROUPS, CHIPS, 2, ROWS, WIDE), BF16),
            pltpu.VMEM((GROUPS, CHIPS, ROWS, WIDE), BF16),
            pltpu.VMEM(piece, BF16),
            pltpu.VMEM(piece, BF16),
            pltpu.VMEM(piece, BF16),
            pltpu.VMEM(piece, BF16),
            pltpu.VMEM(piece, BF16),
            pltpu.VMEM(piece, BF16),
            pltpu.VMEM((BANDS, 16, 128), BF16),
            pltpu.VMEM((BANDS, 16, 128), BF16),
            dma((GROUPS,)),
            dma, dma((GROUPS,)),
            dma((GROUPS,)), dma((GROUPS,)), dma((GROUPS,)), dma((GROUPS,)), dma((GROUPS,)),
            dma((GROUPS,)), dma((GROUPS,)),
            dma((GROUPS,)), dma((GROUPS,)),
            dma((GROUPS,)), dma((GROUPS,)),
            dma((GROUPS,)), dma((GROUPS,)),
            dma, dma,
        ],
        compiler_params=pltpu.CompilerParams(
            collective_id=0, has_side_effects=True, vmem_limit_bytes=40 * 1024 * 1024
        ),
        name="spectral_step",
    )(
        fourier,
        cycle_points.reshape(1, -1),
        lat_weight.reshape(1, -1),
        wave_m.reshape(1, -1),
        legendre.reshape(SLOTS * DEG, GROUPS * WIDE),
        diffusion.reshape(1, -1),
        mode_forward,
        mode_back,
        mode_depth.reshape(1, -1),
    )


def solution(mesh):
    placed = (
        P("lev", None, "band", None),
        P("band"),
        P("band"),
        P(),
        P("band", "lev", None),
        P(),
        P(),
        P(),
        P(),
    )
    return jax.shard_map(
        on_device,
        mesh=mesh,
        in_specs=placed,
        out_specs=P("lev", None, "band", None),
        check_vma=False,
    )
```

time: 227 us -> 71.7 us (0.32)
  the two profiles are of different devices: /device:TPU:1 before, /device:TPU:8 now
where the time goes in v1:
time: 71.7 us; the launch traced here: 71.4 us
  Pallas kernels  63.1 us (88%)
  local copies, waits for them, and re-layouts  8.24 us (11%)
    pallas_call x1, Pallas kernels, on_device(): pl.pallas_call(kernel, out_shape=jax.ShapeDtypeStruct(fourier.shape, BF16...  63.1 us
    unnamed x19, local copies, waits for them, and re-layouts  8.24 us

profile of v1, /device:TPU:8, one launch (start us, length us, event | category | flops | bytes accessed | tf_op | source)
XLA Modules:
  0.0 71.4 jit_solution(12322197684504426624)
XLA Ops:
  0.0 0.0 copy-start
  0.0 1.9 %copy-done = bf16[4,160,2560]{2,1,0:T(8,128)(2,1)S(1)} copy-done((bf16[4,160,2560]{2,1,0:T(8,128)(2,1)S(1)}, bf16[4,160,2560]{2,1,0:T(8,128)(2,1)}, u32[]{:S(2)}) %copy-start) | copy-done | bytes 3276824
  1.9 0.0 copy-start.1
  1.9 0.9 %copy-done.1 = bf16[3,4,40,256]{3,2,1,0:T(8,128)(2,1)S(1)} copy-done((bf16[3,4,40,256]{3,2,1,0:T(8,128)(2,1)S(1)}, bf16[3,4,40,256]{3,2,1,0:T(8,128)(2,1)}, u32[]{:S(2)}) %copy-start.1) | copy-done | bytes 245784
  2.9 0.0 copy-start.2
  2.9 0.7 copy-done.2
  3.6 0.0 copy-start.3
  3.6 0.7 copy-done.3
  4.3 0.0 copy-start.4
  4.3 0.7 copy-done.4
  4.9 0.0 copy-start.5
  4.9 0.7 copy-done.5
  5.6 0.0 copy-start.6
  5.6 0.7 copy-done.6
  6.2 0.0 copy-start.7
  6.2 0.7 copy-done.7
  6.9 0.0 copy-start.8
  6.9 0.7 copy-done.8
  7.6 63.1 %spectral_step.1 = bf16[3,4,40,256]{3,2,1,0:T(8,128)(2,1)S(1)} custom-call(bf16[3,4,40,256]{3,2,1,0:T(8,128)(2,1)S(1)} %copy-done.1, s32[1,40]{1,0:T(1,128)S(1)} %bitcast.8, f32[1,40]{1,0:T(1,128)S(1)} %bitcast.9, s32[1,256]{1,0:T(1,128)S(1)} %bitcast.7, bf16[640,2560]{1,0:T(8,128)(2,1)S(1)} %bitcast.6, f32[1,24]{1,0:T(1,128)S(1)} %bitcast.10, ...), custom_call_target="tpu_custom_call" | custom-call | tf_op jit(solution)/shard_map/spectral_step/pallas_call | solution.py:353
  70.7 0.7 copy.11
Async XLA Ops:
  0.0 1.9 %copy-start = (bf16[4,160,2560]{2,1,0:T(8,128)(2,1)S(1)}, bf16[4,160,2560]{2,1,0:T(8,128)(2,1)}, u32[]{:S(2)}) copy-start(bf16[4,160,2560]{2,1,0:T(8,128)(2,1)} %param.13) | copy-start | bytes 9830404
  1.9 0.9 %copy-start.1 = (bf16[3,4,40,256]{3,2,1,0:T(8,128)(2,1)S(1)}, bf16[3,4,40,256]{3,2,1,0:T(8,128)(2,1)}, u32[]{:S(2)}) copy-start(bf16[3,4,40,256]{3,2,1,0:T(8,128)(2,1)} %four.1) | copy-start | bytes 737284
  2.9 0.7 copy-start.2
  3.6 0.7 copy-start.3
  4.3 0.7 copy-start.4
  4.9 0.7 copy-start.5
  5.6 0.7 copy-start.6
  6.2 0.7 copy-start.7
  6.9 0.7 copy-start.8

commit v2 on v1

--- a/solution.py
+++ b/solution.py
@@ -18,6 +18,7 @@
 CHIPS = 4
 GROUP = 16
 GROUPS = 4
+DIRECT = 3
 WIDE = GROUP * CYC
 ROWS = 48
 DEG = 160
@@ -35,8 +36,8 @@
 
 
 def kernel(
-    four, cyc, latw, wave, leg_hbm, diff, mf, mb, depth, out,
-    leg, tmp, send, r1, xall, acc, ut, gf, gb, grecv,
+    four_hbm, cyc_hbm, latw_hbm, wave_hbm, leg_hbm, diff_hbm, mf_hbm, mb_hbm, depth_hbm, out,
+    four, cyc, latw, wave, diff, mf, mb, depth, in_sem, leg, tmp, send, r1, xall, acc, ut, gf, gb, grecv,
     t1s, t1r, fms, fmr, fps, fpr, esend, r2,
     leg_sem, r1_send, r1_recv, x_send, l_recv, r_recv, far_recv, sib_recv,
     gx_send, gx_recv, t1_send, t1_recv, fm_send, fm_recv, fp_send, fp_recv,
@@ -61,16 +62,28 @@
     def wait_bytes(ref, sem):
         pltpu.make_async_copy(ref, ref, sem).wait()
 
+    early = [(four_hbm, four), (cyc_hbm, cyc), (latw_hbm, latw), (wave_hbm, wave)]
+    late = [(diff_hbm, diff), (mf_hbm, mf), (mb_hbm, mb), (depth_hbm, depth)]
+    loads = [
+        pltpu.make_async_copy(src, dst, in_sem.at[n]) for n, (src, dst) in enumerate(early + late)
+    ]
+    for load in loads:
+        load.start()
+
     barrier = pltpu.get_barrier_semaphore()
 
-    def greet(i, carry):
-        pl.semaphore_signal(
-            barrier, inc=1, device_id={"band": lax.rem(band + i, BANDS)}, device_id_type=MESH
-        )
-        return carry
-
-    lax.fori_loop(1, BANDS, greet, 0)
-    for other in (right, left, sib):
+    for step in (4, 3, 5, 2, 6, 1, 7, 0):
+        base = lax.rem(band + 8 * step, BANDS)
+
+        def greet(i, carry):
+            other = lax.rem(base + i, BANDS)
+            pl.semaphore_signal(
+                barrier, inc=1, device_id={"band": other}, device_id_type=MESH
+            )
+            return carry
+
+        lax.fori_loop(0 if step else 1, 8, greet, 0, unroll=True)
+    for other in (far, right, left, sib):
         pl.semaphore_signal(barrier, inc=1, device_id={"lev": other}, device_id_type=MESH)
 
     for q in range(GROUPS):
@@ -78,6 +91,8 @@
             leg_hbm.at[:, pl.ds(q * WIDE, WIDE)], leg.at[q], leg_sem.at[q]
         ).start()
 
+    for load in loads[:4]:
+        load.wait()
     half = column_of((cyc[...] // 2).astype(F32), CYC)
     weight = column_of(latw[...], CYC)
     waves = wave[...].astype(F32)
@@ -89,7 +104,7 @@
         tmp[pl.ds(c, 256, stride=4), :] = jnp.concatenate(parts, axis=0).T
     send[...] = tmp[...].reshape(BANDS, 16, 128).astype(BF16)
 
-    pl.semaphore_wait(barrier, BANDS - 1 + 3)
+    pl.semaphore_wait(barrier, BANDS - 1 + 4)
 
     def scatter(i, carry):
         t = i // GROUP
@@ -112,6 +127,8 @@
 
     lax.fori_loop(0, BANDS, scatter, 0)
 
+    for load in loads[4:]:
+        load.wait()
     cols = LEVS * LEV3 * COMP
     rows = LEVS * ROWS
     levels = LEVS * LEV3
@@ -181,6 +198,8 @@
                 mine[pl.ds(16 * l, 16), pl.ds(128 * t, 128)] = value.astype(BF16)
         to_lev(mine, mine, x_send.at[q], l_recv.at[q], right)
         to_lev(mine, mine, x_send.at[q], r_recv.at[q], left)
+        if n >= DIRECT:
+            to_lev(mine, mine, x_send.at[q], far_recv.at[q], far)
         to_lev(mine, mine, x_send.at[q], sib_recv.at[q], sib)
 
     def relay(n):
@@ -188,18 +207,12 @@
         from_left = xall.at[q * LEVS + left]
         from_right = xall.at[q * LEVS + right]
         wait_bytes(from_left, l_recv.at[q])
+        if n < DIRECT and n % 2 == 0:
+            to_lev(from_left, from_left, x_send.at[q], far_recv.at[q], right)
+        to_lev(from_left, from_left, x_send.at[q], sib_recv.at[q], sib)
         wait_bytes(from_right, r_recv.at[q])
-        onward = q % 2
-
-        @pl.when(onward == 0)
-        def _():
-            to_lev(from_left, from_left, x_send.at[q], far_recv.at[q], right)
-
-        @pl.when(onward == 1)
-        def _():
+        if n < DIRECT and n % 2 == 1:
             to_lev(from_right, from_right, x_send.at[q], far_recv.at[q], left)
-
-        to_lev(from_left, from_left, x_send.at[q], sib_recv.at[q], sib)
         to_lev(from_right, from_right, x_send.at[q], sib_recv.at[q], sib)
 
     def relay_far(n):
@@ -211,28 +224,30 @@
     def multiply(n):
         q = turn_of(n)
         wait_bytes(xall.at[pl.ds(0, 4)], sib_recv.at[q])
-        wait_bytes(leg.at[q], leg_sem.at[q])
         fields = xall[pl.ds(q * LEVS, LEVS)].reshape(rows, WIDE)
         term = lax.dot_general(
             fields, leg[q], (((1,), (1,)), ((), ())), preferred_element_type=F32
         )
-
-        @pl.when(n == 0)
-        def _():
-            acc[...] = term
-
-        @pl.when(n > 0)
-        def _():
-            acc[...] += term
-
-    def direct(n, carry):
-        pl.when(n < GROUPS)(lambda: take(n))
-        pl.when((n >= 1) & (n < GROUPS + 1))(lambda: relay(n - 1))
-        pl.when((n >= 2) & (n < GROUPS + 2))(lambda: relay_far(n - 2))
-        pl.when(n >= 3)(lambda: multiply(n - 3))
-        return carry
-
-    lax.fori_loop(0, GROUPS + 3, direct, 0)
+        acc[...] = term if n == 0 else acc[...] + term
+
+    take(0)
+    for q in range(GROUPS):
+        wait_bytes(leg.at[q], leg_sem.at[q])
+    take(1)
+    take(2)
+    relay(0)
+    take(3)
+    relay(1)
+    relay(2)
+    relay_far(0)
+    relay(3)
+    multiply(0)
+    relay_far(1)
+    relay_far(3)
+    multiply(1)
+    relay_far(2)
+    multiply(3)
+    multiply(2)
 
     own_slot = (iota((rows, 1), 0) // COMP) % SLOTS == slot_of
     spectral = jnp.where(own_slot & usable, acc[...], 0.0).astype(BF16)
@@ -242,12 +257,10 @@
     ut[...] = jnp.where(own_slot, updated, 0.0).astype(BF16)
 
     def out_of(n):
-        t = (GROUPS - 1) - n
-        t = t + (t // 2) * (5 - 2 * t)
-        return lax.rem(qme + t, GROUPS)
-
-    def ahead_of(q):
-        sense = 1 + 2 * (q % 2)
+        return lax.rem(qme + (2, 3, 0, 1)[n], GROUPS)
+
+    def ahead_of(n):
+        sense = 1 + 2 * (n % 2)
         ahead = lax.rem(x + sense, CHIPS)
         behind = lax.rem(x + 4 - sense, CHIPS)
         return ahead, behind
@@ -265,16 +278,20 @@
     def first_hop(n):
         q = out_of(n)
         wait_bytes(grecv.at[q], gx_recv.at[q])
-        ahead, behind = ahead_of(q)
+        ahead, behind = ahead_of(n)
         opposite = lax.rem(x + 2, CHIPS)
         t1s[q] = chip_sum(q, opposite).astype(BF16)
-        to_lev(t1s.at[q], t1r.at[q], t1_send.at[q], t1_recv.at[q], ahead * 2 + core)
+        first = far if n >= DIRECT else ahead * 2 + core
+        to_lev(t1s.at[q], t1r.at[q], t1_send.at[q], t1_recv.at[q], first)
         fms[q] = chip_sum(q, behind).astype(BF16)
         to_lev(fms.at[q], fmr.at[q], fm_send.at[q], fm_recv.at[q], behind * 2 + core)
+        if n >= DIRECT:
+            fps[q] = chip_sum(q, ahead).astype(BF16)
+            to_lev(fps.at[q], fpr.at[q], fp_send.at[q], fp_recv.at[q], ahead * 2 + core)
 
     def second_hop(n):
         q = out_of(n)
-        ahead, behind = ahead_of(q)
+        ahead, behind = ahead_of(n)
         wait_bytes(t1r.at[q], t1_recv.at[q])
         fps[q] = (chip_sum(q, ahead) + t1r[q].astype(F32)).astype(BF16)
         to_lev(fps.at[q], fpr.at[q], fp_send.at[q], fp_recv.at[q], ahead * 2 + core)
@@ -284,6 +301,9 @@
         wait_bytes(fmr.at[q], fm_recv.at[q])
         wait_bytes(fpr.at[q], fp_recv.at[q])
         total = chip_sum(q, x) + fmr[q].astype(F32) + fpr[q].astype(F32)
+        if n >= DIRECT:
+            wait_bytes(t1r.at[q], t1_recv.at[q])
+            total = total + t1r[q].astype(F32)
         for i in range(GROUP):
             t, low = divmod(CYC * i, 128)
             value = None
@@ -317,14 +337,21 @@
 
         lax.fori_loop(0, GROUP, deliver, 0)
 
-    def back_transform(n, carry):
-        pl.when(n < GROUPS)(lambda: inverse(n))
-        pl.when((n >= 1) & (n < GROUPS + 1))(lambda: first_hop(n - 1))
-        pl.when((n >= 2) & (n < GROUPS + 2))(lambda: second_hop(n - 2))
-        pl.when(n >= 3)(lambda: give(n - 3))
-        return carry
-
-    lax.fori_loop(0, GROUPS + 3, back_transform, 0)
+    inverse(0)
+    inverse(1)
+    inverse(2)
+    first_hop(0)
+    inverse(3)
+    first_hop(1)
+    first_hop(2)
+    first_hop(3)
+    second_hop(0)
+    second_hop(1)
+    second_hop(2)
+    give(0)
+    give(3)
+    give(1)
+    give(2)
 
     wait_bytes(r2, r2_recv)
     tmp[...] = r2[...].astype(F32).reshape(BANDS * 16, 128)
@@ -353,9 +380,18 @@
     return pl.pallas_call(
         kernel,
         out_shape=jax.ShapeDtypeStruct(fourier.shape, BF16),
-        in_specs=[vmem] * 4 + [pl.BlockSpec(memory_space=pl.ANY)] + [vmem] * 4,
+        in_specs=[pl.BlockSpec(memory_space=pltpu.HBM)] * 9,
         out_specs=vmem,
         scratch_shapes=[
+            pltpu.VMEM((LEV3, COMP, CYC, 256), BF16),
+            pltpu.VMEM((1, CYC), jnp.int32),
+            pltpu.VMEM((1, CYC), F32),
+            pltpu.VMEM((1, 256), jnp.int32),
+            pltpu.VMEM((1, LEVS * LEV3), F32),
+            pltpu.VMEM((LEVS * LEV3, LEVS * LEV3), BF16),
+            pltpu.VMEM((LEVS * LEV3, LEVS * LEV3), BF16),
+            pltpu.VMEM((1, LEVS * LEV3), F32),
+            dma((8,)),
             pltpu.VMEM((GROUPS, SLOTS * DEG, WIDE), BF16),
             pltpu.VMEM((BANDS * 16, 128), F32),
             pltpu.VMEM((BANDS, 16, 128), BF16),
@@ -384,10 +420,10 @@
             dma, dma,
         ],
         compiler_params=pltpu.CompilerParams(
-            collective_id=0, has_side_effects=True, vmem_limit_bytes=40 * 1024 * 1024
+            collective_id=0, has_side_effects=True, vmem_limit_bytes=24 * 1024 * 1024
         ),
         name="spectral_step",
-    )(
+    )(*(pltpu.with_memory_space_constraint(v, pltpu.HBM) for v in (
         fourier,
         cycle_points.reshape(1, -1),
         lat_weight.reshape(1, -1),
@@ -397,7 +433,7 @@
         mode_forward,
         mode_back,
         mode_depth.reshape(1, -1),
-    )
+    )))
 
 
 def solution(mesh):

time: 71.7 us -> 60.9 us (0.85)
  the two profiles are of different devices: /device:TPU:8 before, /device:TPU:1 now
where the time goes in v2:
time: 60.9 us; the launch traced here: 60.6 us
  Pallas kernels  59.9 us (98%)
  local copies, waits for them, and re-layouts  0.7 us (1%)
    pallas_call x1, Pallas kernels, on_device(): pl.pallas_call(kernel, out_shape=jax.ShapeDtypeStruct(fourier.shape, BF16...  59.9 us

profile of v2, /device:TPU:1, one launch (start us, length us, event | category | flops | bytes accessed | tf_op | source)
XLA Modules:
  0.0 60.6 jit_solution(3413577965087753545)
XLA Ops:
  0.0 59.9 %spectral_step.1 = bf16[3,4,40,256]{3,2,1,0:T(8,128)(2,1)S(1)} custom-call(bf16[3,4,40,256]{3,2,1,0:T(8,128)(2,1)} %four_hbm.1, s32[1,40]{1,0:T(1,128)} %bitcast.8, f32[1,40]{1,0:T(1,128)} %bitcast.9, s32[1,256]{1,0:T(1,128)} %bitcast.7, bf16[640,2560]{1,0:T(8,128)(2,1)} %bitcast.6, f32[1,24]{1,0:T(1,128)} %bitcast.10, bf16[24,24]{1,0:T(8,128)(2,1)} %mf_hbm.1, ...), custom_call_target="tpu_custom_call" | custom-call | tf_op jit(solution)/shard_map/spectral_step/pallas_call | solution.py:380
  59.9 0.7 %copy.11 = bf16[3,4,40,256]{3,2,1,0:T(8,128)(2,1)} copy(bf16[3,4,40,256]{3,2,1,0:T(8,128)(2,1)S(1)} %spectral_step.1) | data formatting | bytes 491520

commit v3 on v2

--- a/solution.py
+++ b/solution.py
@@ -24,6 +24,7 @@
 DEG = 160
 SLOTS = 4
 NSPEC = 1280
+OUT_TURN = (2, 3, 0, 1)
 
 
 def iota(shape, dim):
@@ -106,26 +107,23 @@
 
     pl.semaphore_wait(barrier, BANDS - 1 + 4)
 
-    def scatter(i, carry):
-        t = i // GROUP
-        turn = t + (t // 2) * (5 - 2 * t)
-        there = lax.rem(qme + 4 - turn, GROUPS) * GROUP + lax.rem(band + i, GROUP)
-
-        @pl.when(there != band)
-        def _():
+    def send_tiles(turn, src, dst, s_sem, r_sem):
+        base = lax.rem(qme + turn, GROUPS) * GROUP
+
+        def one(i, carry):
+            there = base + lax.rem(band + i, GROUP)
             pltpu.make_async_remote_copy(
-                src_ref=send.at[there], dst_ref=r1.at[band],
-                send_sem=r1_send, recv_sem=r1_recv.at[qme],
+                src_ref=src.at[there], dst_ref=dst.at[band], send_sem=s_sem, recv_sem=r_sem,
                 device_id={"band": there}, device_id_type=MESH,
             ).start()
-
-        @pl.when(there == band)
-        def _():
-            pltpu.make_async_copy(send.at[band], r1.at[band], r1_recv.at[qme]).start()
-
-        return carry
-
-    lax.fori_loop(0, BANDS, scatter, 0)
+            return carry
+
+        lax.fori_loop(0 if turn else 1, GROUP, one, 0, unroll=True)
+        if turn == 0:
+            pltpu.make_async_copy(src.at[band], dst.at[band], r_sem).start()
+
+    for turn in (0, 3, 1, 2):
+        send_tiles(turn, send, r1, r1_send, r1_recv.at[qme])
 
     for load in loads[4:]:
         load.wait()
@@ -177,13 +175,12 @@
     lane16 = iota((16, 128), 1)
 
     def turn_of(n):
-        t = n + (n // 2) * (5 - 2 * n)
-        return lax.rem(qme + t, GROUPS)
+        return lax.rem(qme + (0, 1, 3, 2)[n], GROUPS)
 
     def take(n):
         q = turn_of(n)
         wait_bytes(r1.at[pl.ds(q * GROUP, GROUP)], r1_recv.at[q])
-        mine = xall.at[q * LEVS + lev]
+        mine = xall.at[q * CHIPS + x, core]
         tiles = [r1[q * GROUP + i].astype(F32) for i in range(GROUP)]
         for l in range(LEV3):
             for t in range(WIDE // 128):
@@ -196,39 +193,58 @@
                     moved = pltpu.roll(tiles[i], shift, 1) if shift else tiles[i]
                     value = moved if value is None else jnp.where(lane16 >= low, moved, value)
                 mine[pl.ds(16 * l, 16), pl.ds(128 * t, 128)] = value.astype(BF16)
-        to_lev(mine, mine, x_send.at[q], l_recv.at[q], right)
-        to_lev(mine, mine, x_send.at[q], r_recv.at[q], left)
+        for part in range(LEV3):
+            level = mine.at[pl.ds(16 * part, 16)]
+            to_lev(level, level, x_send.at[q], l_recv.at[q, part], right)
+            to_lev(level, level, x_send.at[q], r_recv.at[q, part], left)
         if n >= DIRECT:
             to_lev(mine, mine, x_send.at[q], far_recv.at[q], far)
         to_lev(mine, mine, x_send.at[q], sib_recv.at[q], sib)
 
     def relay(n):
         q = turn_of(n)
-        from_left = xall.at[q * LEVS + left]
-        from_right = xall.at[q * LEVS + right]
-        wait_bytes(from_left, l_recv.at[q])
-        if n < DIRECT and n % 2 == 0:
-            to_lev(from_left, from_left, x_send.at[q], far_recv.at[q], right)
+        from_left = xall.at[q * CHIPS + lax.rem(x + 3, CHIPS), core]
+        from_right = xall.at[q * CHIPS + lax.rem(x + 1, CHIPS), core]
+        for part in range(LEV3):
+            level = from_left.at[pl.ds(16 * part, 16)]
+            wait_bytes(level, l_recv.at[q, part])
+            if n < DIRECT and n % 2 == 0:
+                to_lev(level, level, x_send.at[q], far_recv.at[q], right)
         to_lev(from_left, from_left, x_send.at[q], sib_recv.at[q], sib)
-        wait_bytes(from_right, r_recv.at[q])
-        if n < DIRECT and n % 2 == 1:
-            to_lev(from_right, from_right, x_send.at[q], far_recv.at[q], left)
+        for part in range(LEV3):
+            level = from_right.at[pl.ds(16 * part, 16)]
+            wait_bytes(level, r_recv.at[q, part])
+            if n < DIRECT and n % 2 == 1:
+                to_lev(level, level, x_send.at[q], far_recv.at[q], left)
         to_lev(from_right, from_right, x_send.at[q], sib_recv.at[q], sib)
 
     def relay_far(n):
         q = turn_of(n)
-        from_far = xall.at[q * LEVS + far]
+        from_far = xall.at[q * CHIPS + lax.rem(x + 2, CHIPS), core]
         wait_bytes(from_far, far_recv.at[q])
         to_lev(from_far, from_far, x_send.at[q], sib_recv.at[q], sib)
 
+    def term_of(fields, q):
+        return lax.dot_general(
+            fields.reshape(-1, WIDE), leg[q], (((1,), (1,)), ((), ())),
+            preferred_element_type=F32,
+        )
+
     def multiply(n):
         q = turn_of(n)
-        wait_bytes(xall.at[pl.ds(0, 4)], sib_recv.at[q])
-        fields = xall[pl.ds(q * LEVS, LEVS)].reshape(rows, WIDE)
-        term = lax.dot_general(
-            fields, leg[q], (((1,), (1,)), ((), ())), preferred_element_type=F32
-        )
+        wait_bytes(xall.at[pl.ds(0, 2)], sib_recv.at[q])
+        term = term_of(xall[pl.ds(q * CHIPS, CHIPS)], q).reshape(acc.shape)
         acc[...] = term if n == 0 else acc[...] + term
+
+    def multiply_plane(n, plane):
+        q = turn_of(n)
+        term = term_of(xall[pl.ds(q * CHIPS, CHIPS), plane], q)
+        acc[:, plane] += term.reshape(CHIPS, ROWS, SLOTS * DEG)
+
+    def multiply_last(n):
+        multiply_plane(n, core)
+        wait_bytes(xall.at[pl.ds(0, 2)], sib_recv.at[turn_of(n)])
+        multiply_plane(n, 1 - core)
 
     take(0)
     for q in range(GROUPS):
@@ -247,17 +263,17 @@
     multiply(1)
     relay_far(2)
     multiply(3)
-    multiply(2)
+    multiply_last(2)
 
     own_slot = (iota((rows, 1), 0) // COMP) % SLOTS == slot_of
-    spectral = jnp.where(own_slot & usable, acc[...], 0.0).astype(BF16)
+    spectral = jnp.where(own_slot & usable, acc[...].reshape(rows, SLOTS * DEG), 0.0).astype(BF16)
     modes = jnp.dot(forward, spectral, preferred_element_type=F32)
     scaled = (modes / damping).astype(BF16)
     updated = jnp.dot(backward, scaled, preferred_element_type=F32)
-    ut[...] = jnp.where(own_slot, updated, 0.0).astype(BF16)
+    ut[...] = jnp.where(own_slot, updated, 0.0).astype(BF16).reshape(ut.shape)
 
     def out_of(n):
-        return lax.rem(qme + (2, 3, 0, 1)[n], GROUPS)
+        return lax.rem(qme + OUT_TURN[n], GROUPS)
 
     def ahead_of(n):
         sense = 1 + 2 * (n % 2)
@@ -267,13 +283,26 @@
 
     def inverse(n):
         q = out_of(n)
-        sums = jnp.dot(ut[...], leg[q], preferred_element_type=F32)
-        gf[q] = sums.reshape(LEVS, ROWS, WIDE)
-        gb[q] = sums.astype(BF16).reshape(CHIPS, 2, ROWS, WIDE)
+        if n == 0:
+            theirs = jnp.dot(
+                ut[:, 1 - core].reshape(-1, SLOTS * DEG), leg[q], preferred_element_type=F32
+            )
+            gb[q, :, 1 - core] = theirs.astype(BF16).reshape(CHIPS, ROWS, WIDE)
+        else:
+            sums = jnp.dot(
+                ut[...].reshape(rows, SLOTS * DEG), leg[q], preferred_element_type=F32
+            )
+            gf[q] = sums.reshape(CHIPS, 2, ROWS, WIDE)
+            gb[q] = sums.astype(BF16).reshape(CHIPS, 2, ROWS, WIDE)
         to_lev(gb.at[q, :, 1 - core], grecv.at[q], gx_send.at[q], gx_recv.at[q], sib)
+        if n == 0:
+            mine = jnp.dot(
+                ut[:, core].reshape(-1, SLOTS * DEG), leg[q], preferred_element_type=F32
+            )
+            gf[q, :, core] = mine.reshape(CHIPS, ROWS, WIDE)
 
     def chip_sum(q, target):
-        return gf[q, target * 2 + core] + grecv[q, target].astype(F32)
+        return gf[q, target, core] + grecv[q, target].astype(F32)
 
     def first_hop(n):
         q = out_of(n)
@@ -282,7 +311,9 @@
         opposite = lax.rem(x + 2, CHIPS)
         t1s[q] = chip_sum(q, opposite).astype(BF16)
         first = far if n >= DIRECT else ahead * 2 + core
-        to_lev(t1s.at[q], t1r.at[q], t1_send.at[q], t1_recv.at[q], first)
+        for part in range(LEV3):
+            at = pl.ds(16 * part, 16)
+            to_lev(t1s.at[q, at], t1r.at[q, at], t1_send.at[q], t1_recv.at[q, part], first)
         fms[q] = chip_sum(q, behind).astype(BF16)
         to_lev(fms.at[q], fmr.at[q], fm_send.at[q], fm_recv.at[q], behind * 2 + core)
         if n >= DIRECT:
@@ -292,9 +323,14 @@
     def second_hop(n):
         q = out_of(n)
         ahead, behind = ahead_of(n)
-        wait_bytes(t1r.at[q], t1_recv.at[q])
-        fps[q] = (chip_sum(q, ahead) + t1r[q].astype(F32)).astype(BF16)
-        to_lev(fps.at[q], fpr.at[q], fp_send.at[q], fp_recv.at[q], ahead * 2 + core)
+        for part in range(LEV3):
+            at = pl.ds(16 * part, 16)
+            wait_bytes(t1r.at[q, at], t1_recv.at[q, part])
+            mine = gf[q, ahead, core, at] + grecv[q, ahead, at].astype(F32)
+            fps[q, at] = (mine + t1r[q, at].astype(F32)).astype(BF16)
+            to_lev(
+                fps.at[q, at], fpr.at[q, at], fp_send.at[q], fp_recv.at[q], ahead * 2 + core
+            )
 
     def give(n):
         q = out_of(n)
@@ -302,7 +338,8 @@
         wait_bytes(fpr.at[q], fp_recv.at[q])
         total = chip_sum(q, x) + fmr[q].astype(F32) + fpr[q].astype(F32)
         if n >= DIRECT:
-            wait_bytes(t1r.at[q], t1_recv.at[q])
+            for part in range(LEV3):
+                wait_bytes(t1r.at[q, pl.ds(16 * part, 16)], t1_recv.at[q, part])
             total = total + t1r[q].astype(F32)
         for i in range(GROUP):
             t, low = divmod(CYC * i, 128)
@@ -318,24 +355,7 @@
                 value = moved if value is None else jnp.where(lane16 >= CYC * l, moved, value)
             esend[q * GROUP + i] = value.astype(BF16)
 
-        def deliver(i, carry):
-            there = q * GROUP + lax.rem(band + i, GROUP)
-
-            @pl.when(there != band)
-            def _():
-                pltpu.make_async_remote_copy(
-                    src_ref=esend.at[there], dst_ref=r2.at[band],
-                    send_sem=e_send, recv_sem=r2_recv,
-                    device_id={"band": there}, device_id_type=MESH,
-                ).start()
-
-            @pl.when(there == band)
-            def _():
-                pltpu.make_async_copy(esend.at[band], r2.at[band], r2_recv).start()
-
-            return carry
-
-        lax.fori_loop(0, GROUP, deliver, 0)
+        send_tiles(OUT_TURN[n], esend, r2, e_send, r2_recv)
 
     inverse(0)
     inverse(1)
@@ -363,7 +383,8 @@
     wait_bytes(send.at[pl.ds(0, BANDS - 1)], r1_send)
     wait_bytes(esend.at[pl.ds(0, BANDS - 1)], e_send)
     for q in range(GROUPS):
-        wait_bytes(xall.at[pl.ds(0, 7)], x_send.at[q])
+        wait_bytes(xall.at[pl.ds(0, 3)], x_send.at[q])
+        wait_bytes(xall.at[0, 0], x_send.at[q])
         wait_bytes(grecv.at[q], gx_send.at[q])
         wait_bytes(t1s.at[q], t1_send.at[q])
         wait_bytes(fms.at[q], fm_send.at[q])
@@ -396,10 +417,10 @@
             pltpu.VMEM((BANDS * 16, 128), F32),
             pltpu.VMEM((BANDS, 16, 128), BF16),
             pltpu.VMEM((BANDS, 16, 128), BF16),
-            pltpu.VMEM((GROUPS * LEVS, ROWS, WIDE), BF16),
-            pltpu.VMEM((LEVS * ROWS, SLOTS * DEG), F32),
-            pltpu.VMEM((LEVS * ROWS, SLOTS * DEG), BF16),
-            pltpu.VMEM((GROUPS, LEVS, ROWS, WIDE), F32),
+            pltpu.VMEM((GROUPS * CHIPS, 2, ROWS, WIDE), BF16),
+            pltpu.VMEM((CHIPS, 2, ROWS, SLOTS * DEG), F32),
+            pltpu.VMEM((CHIPS, 2, ROWS, SLOTS * DEG), BF16),
+            pltpu.VMEM((GROUPS, CHIPS, 2, ROWS, WIDE), F32),
             pltpu.VMEM((GROUPS, CHIPS, 2, ROWS, WIDE), BF16),
             pltpu.VMEM((GROUPS, CHIPS, ROWS, WIDE), BF16),
             pltpu.VMEM(piece, BF16),
@@ -412,9 +433,10 @@
             pltpu.VMEM((BANDS, 16, 128), BF16),
             dma((GROUPS,)),
             dma, dma((GROUPS,)),
-            dma((GROUPS,)), dma((GROUPS,)), dma((GROUPS,)), dma((GROUPS,)), dma((GROUPS,)),
+            dma((GROUPS,)), dma((GROUPS, LEV3)), dma((GROUPS, LEV3)),
             dma((GROUPS,)), dma((GROUPS,)),
             dma((GROUPS,)), dma((GROUPS,)),
+            dma((GROUPS,)), dma((GROUPS, LEV3)),
             dma((GROUPS,)), dma((GROUPS,)),
             dma((GROUPS,)), dma((GROUPS,)),
             dma, dma,

time: 60.9 us -> 61.3 us (level)
  no operation moved by 1% of the time
where the time goes in v3:
time: 61.3 us; the launch traced here: 61.2 us
  Pallas kernels  60.5 us (99%)
  local copies, waits for them, and re-layouts  0.7 us (1%)
    pallas_call x1, Pallas kernels, on_device(): pl.pallas_call(kernel, out_shape=jax.ShapeDtypeStruct(fourier.shape, BF16...  60.5 us

profile of v3, /device:TPU:1, one launch (start us, length us, event | category | flops | bytes accessed | tf_op | source)
XLA Modules:
  0.0 61.2 jit_solution(16419821188745486107)
XLA Ops:
  0.0 60.5 %spectral_step.1 = bf16[3,4,40,256]{3,2,1,0:T(8,128)(2,1)S(1)} custom-call(bf16[3,4,40,256]{3,2,1,0:T(8,128)(2,1)} %four_hbm.1, s32[1,40]{1,0:T(1,128)} %bitcast.8, f32[1,40]{1,0:T(1,128)} %bitcast.9, s32[1,256]{1,0:T(1,128)} %bitcast.7, bf16[640,2560]{1,0:T(8,128)(2,1)} %bitcast.6, f32[1,24]{1,0:T(1,128)} %bitcast.10, bf16[24,24]{1,0:T(8,128)(2,1)} %mf_hbm.1, ...), custom_call_target="tpu_custom_call" | custom-call | tf_op jit(solution)/shard_map/spectral_step/pallas_call | solution.py:401
  60.5 0.7 %copy.11 = bf16[3,4,40,256]{3,2,1,0:T(8,128)(2,1)} copy(bf16[3,4,40,256]{3,2,1,0:T(8,128)(2,1)S(1)} %spectral_step.1) | data formatting | bytes 491520
